TPU v7x, 32 devices: a whole 2x2x4 slice. The times are simulated.
32 devices in a mesh: pipe: 4 (over y, x), ctx: 8 (over z, core).
Axes of the slice: x: 2, y: 2, z: 4, core: 2. Of those that a mesh axis runs over, the one named last changes fastest.
Arguments:
- x_in: bfloat16 [4, 512, 8192], P('pipe', 'ctx'), may hold values from -6 to 6
- z_in: bfloat16 [4, 512, 8192], P('pipe', 'ctx'), may hold values from -6 to 6
- bc_in: bfloat16 [4, 512, 1024], P('pipe', 'ctx'), may hold values from -6 to 6
- dt_raw: bfloat16 [4, 512, 128], P('pipe', 'ctx'), may hold values from -3.2 to 3.2
- a_log: float32 [4, 128], P('pipe'), may hold values from -12 to 3
- dt_bias: float32 [4, 128], P('pipe'), may hold values from -3.8 to -3
- d_skip: float32 [4, 128], P('pipe'), may hold values from 0.5 to 1.5
- conv_x: bfloat16 [4, 4, 8192], P('pipe'), may hold values from -3 to 3
- conv_bc: bfloat16 [4, 4, 1024], P('pipe'), may hold values from -3 to 3
- norm_gain: float32 [4, 8192], P('pipe'), may hold values from 0.5 to 1.5
- seg_ids: int32 [4, 512], P('pipe', 'ctx'), may hold values from 0 to 3, never falling along the last dimension, each value on 1 to 256 neighbouring positions
- query: bfloat16 [4, 512, 2048], P('pipe', 'ctx'), may hold values from -192 to 192
- keys: bfloat16 [4, 512, 256], P('pipe', 'ctx'), may hold values from -6 to 6
- values: bfloat16 [4, 512, 256], P('pipe', 'ctx'), may hold values from -6 to 6
Outputs:
- mamba_out: bfloat16 [4, 512, 8192], P('pipe', 'ctx')
- handoff: bfloat16 [4, 512, 2048], P('pipe', 'ctx')
Inputs may be any that keep to these rules, and one draw needn't show every extreme that they name: `seg_ids`: segment numbers never fall along a section's sequence; no segment is longer than 256 positions, and one has exactly that many.
All inputs are finite; a program needn't handle non-finite values.
Results may differ from a plain program's by a relative error of at most 0.0044.
The roundings to bfloat16 on the way count: a program that leaves them out, or rounds other values in their place, can miss the bound.
Values may be sent and summed in bfloat16 or wider, within the bound.
No kernel may reach another device: no remote copies, remote signals or barrier semaphores. Data moves between devices by JAX's collectives and lax.ppermute only.
A program may use at most 128 MiB of HBM per device.

v0:
```python
import math
import jax
import jax.numpy as jnp
from jax import lax
from jax.sharding import PartitionSpec as P

G = 4
AH = 32
KVH = 4
HD = 64
norm_eps = 1e-05


def from_behind(value, axis, steps):
    count = lax.axis_size(axis)
    pairs = [(source, (source + steps) % count) for source in range(count)]
    return lax.ppermute(value, axis, pairs)


def causal_taps(rim, inputs, rim_ids, ids, weights):
    lag = rim.shape[0]
    length = inputs.shape[0]
    padded = jnp.concatenate([rim, inputs], axis=0)
    padded_ids = jnp.concatenate([rim_ids, ids])
    layout = (length,) + (1,) * (inputs.ndim - 1)
    summed = jnp.zeros(inputs.shape, jnp.float32)
    for tap in range(lag + 1):
        same = (padded_ids[tap : tap + length] == ids).reshape(layout)
        summed = summed + jnp.where(
            same,
            weights[tap].astype(jnp.float32) * padded[tap : tap + length].astype(jnp.float32),
            0.0,
        )
    return jax.nn.silu(summed).astype(jnp.bfloat16)


def per_head(grouped, heads):
    leading = grouped.shape[:-3]
    groups = grouped.shape[-2]
    states = grouped.shape[-1]
    moved = jnp.swapaxes(grouped, -3, -2)
    spread = jnp.repeat(moved, heads // groups, axis=-3)
    return spread.reshape(leading + (heads, 2 * states))


def state_space(x_conv, bc_conv, step_size, rates, skip, ids):
    length, local_heads, head_dim = x_conv.shape
    states = bc_conv.shape[2] // 2
    span = min(256, length)
    blocks = length // span
    lower = jnp.arange(span)[:, None] >= jnp.arange(span)[None, :]

    def advance(carry, item):
        memory, last_id = carry
        x_block, bc_block, step_block, id_block = item
        b_part = bc_block[:, :, :states]
        c_part = bc_block[:, :, states:]
        logs = jnp.cumsum(step_block * rates[None, :], axis=0)
        allowed = lower & (id_block[:, None] == id_block[None, :])
        gaps = logs[:, None, :] - logs[None, :, :]
        weights = (
            jnp.where(allowed[:, :, None], jnp.exp(jnp.minimum(gaps, 0.0)), 0.0)
            * step_block[None, :, :]
        )
        inner = jnp.einsum("thn,shn->tsh", c_part, b_part, preferred_element_type=jnp.float32)
        mixing = (inner * weights).astype(jnp.bfloat16)
        local_part = jnp.einsum("tsh,shp->thp", mixing, x_block, preferred_element_type=jnp.float32)
        keep = jnp.where((id_block == last_id)[:, None], jnp.exp(logs), 0.0)
        carried = (
            jnp.einsum(
                "thn,hpn->thp", c_part.astype(jnp.float32), memory, precision=lax.Precision.HIGHEST
            )
            * keep[:, :, None]
        )
        result = local_part + carried + skip[None, :, None] * x_block.astype(jnp.float32)
        tail = logs[span - 1]
        writes = (
            jnp.where((id_block == id_block[span - 1])[:, None], jnp.exp(tail[None, :] - logs), 0.0)
            * step_block
        )
        scaled = (x_block.astype(jnp.float32) * writes[:, :, None]).astype(jnp.bfloat16)
        added = jnp.einsum("shp,shn->hpn", scaled, b_part, preferred_element_type=jnp.float32)
        kept = jnp.where(id_block[span - 1] == last_id, jnp.exp(tail), 0.0)
        memory = memory * kept[:, None, None] + added
        return ((memory, id_block[span - 1]), result)

    start = (jnp.zeros((local_heads, head_dim, states), jnp.float32), jnp.array(-1, jnp.int32))
    items = (
        x_conv.reshape(blocks, span, local_heads, head_dim),
        bc_conv.reshape(blocks, span, local_heads, 2 * states),
        step_size.reshape(blocks, span, local_heads),
        ids.reshape(blocks, span),
    )
    (memory, _), outputs = lax.scan(advance, start, items)
    return (memory, outputs.reshape(length, local_heads, head_dim))


def on_device(
    x_in,
    z_in,
    bc_in,
    dt_raw,
    a_log,
    dt_bias,
    d_skip,
    conv_x,
    conv_bc,
    norm_gain,
    seg_ids,
    query,
    keys,
    values,
):
    ranks = lax.axis_size("ctx")
    place = lax.axis_index("ctx")
    tokens_here = x_in.shape[1]
    heads = dt_raw.shape[2]
    head_dim = x_in.shape[2] // heads
    states = bc_in.shape[2] // (2 * G)
    lag = conv_x.shape[1] - 1
    own_ids = seg_ids[0]
    all_ids = lax.all_gather(own_ids, "ctx", axis=0, tiled=True)
    local_heads = heads // ranks
    first_head = place * local_heads
    x_send = x_in[0].reshape(tokens_here, heads, head_dim)
    bc_send = per_head(bc_in[0].reshape(tokens_here, 2, G, states), heads)
    x_heads, raw_heads, bc_heads = (
        lax.all_to_all(x_send, "ctx", split_axis=1, concat_axis=0, tiled=True),
        lax.all_to_all(dt_raw[0], "ctx", split_axis=1, concat_axis=0, tiled=True),
        lax.all_to_all(bc_send, "ctx", split_axis=1, concat_axis=0, tiled=True),
    )
    empty_ids = jnp.full((lag,), -1, jnp.int32)
    taps_x = lax.dynamic_slice_in_dim(
        conv_x[0].reshape(lag + 1, heads, head_dim), first_head, local_heads, 1
    )
    taps_bc = lax.dynamic_slice_in_dim(
        per_head(conv_bc[0].reshape(lag + 1, 2, G, states), heads), first_head, local_heads, 1
    )
    x_conv = causal_taps(
        jnp.zeros((lag,) + x_heads.shape[1:], jnp.bfloat16), x_heads, empty_ids, all_ids, taps_x
    )
    bc_conv = causal_taps(
        jnp.zeros((lag,) + bc_heads.shape[1:], jnp.bfloat16), bc_heads, empty_ids, all_ids, taps_bc
    )
    bias_heads = lax.dynamic_slice_in_dim(dt_bias[0], first_head, local_heads)
    rates = -jnp.exp(lax.dynamic_slice_in_dim(a_log[0], first_head, local_heads))
    skip = lax.dynamic_slice_in_dim(d_skip[0], first_head, local_heads)
    step_size = jax.nn.softplus(raw_heads.astype(jnp.float32) + bias_heads[None, :])
    _, local = state_space(x_conv, bc_conv, step_size, rates, skip, all_ids)
    attention_mixture = local.astype(jnp.bfloat16)
    mixed_tokens = lax.all_to_all(
        attention_mixture, "ctx", split_axis=0, concat_axis=1, tiled=True
    ).reshape(tokens_here, heads * head_dim)
    gated = mixed_tokens.astype(jnp.float32) * jax.nn.silu(z_in[0].astype(jnp.float32))
    grouped = gated.reshape(tokens_here, G, heads * head_dim // G)
    factor = lax.rsqrt(jnp.mean(grouped * grouped, axis=-1, keepdims=True) + norm_eps)
    mamba_out = (
        (grouped * factor).reshape(tokens_here, heads * head_dim) * norm_gain[0][None, :]
    ).astype(jnp.bfloat16)
    ratio = AH // KVH
    queries = query[0].reshape(tokens_here, KVH, ratio, HD)
    query_pos = place * tokens_here + jnp.arange(tokens_here)
    logit_scale = 1.0 / math.sqrt(HD)
    initial = (
        jnp.full((KVH, ratio, tokens_here), -1e30, jnp.float32),
        jnp.zeros((KVH, ratio, tokens_here), jnp.float32),
        jnp.zeros((KVH, ratio, tokens_here, HD), jnp.float32),
    )
    carry = initial
    key_piece = lax.all_gather(keys[0], "ctx", axis=0, tiled=True)
    value_piece = lax.all_gather(values[0], "ctx", axis=0, tiled=True)
    count = key_piece.shape[0]
    width = math.gcd(count, 512)
    key_blocks = key_piece.reshape(count // width, width, KVH, HD)
    value_blocks = value_piece.reshape(count // width, width, KVH, HD)

    def visit(running, item):
        key_block, value_block, order = item
        first = order * width
        key_ids = lax.dynamic_slice_in_dim(all_ids, first, width)
        key_pos = first + jnp.arange(width)
        allowed = (query_pos[:, None] >= key_pos[None, :]) & (own_ids[:, None] == key_ids[None, :])
        largest, totals, accum = running
        attention_logits = (
            jnp.einsum("tgrd,mgd->grtm", queries, key_block, preferred_element_type=jnp.float32)
            * logit_scale
        )
        masked = jnp.where(allowed, attention_logits, -1e30)
        newest = jnp.maximum(largest, jnp.max(masked, axis=-1))
        weight = jnp.where(allowed, jnp.exp(masked - newest[..., None]), 0.0)
        correct = jnp.exp(largest - newest)
        totals = totals * correct + jnp.sum(weight, axis=-1)
        accum = accum * correct[..., None] + jnp.einsum(
            "grtm,mgd->grtd",
            weight.astype(jnp.bfloat16),
            value_block,
            preferred_element_type=jnp.float32,
        )
        running = (newest, totals, accum)
        return (running, None)

    carry, _ = lax.scan(
        visit, carry, (key_blocks, value_blocks, jnp.arange(count // width, dtype=jnp.int32))
    )
    largest, totals, accum = carry
    attended = accum / totals[..., None]
    attended = (
        jnp.transpose(attended, (2, 0, 1, 3)).reshape(tokens_here, AH * HD).astype(jnp.bfloat16)
    )
    handoff = from_behind(attended, "pipe", 1)
    return (mamba_out[None], handoff[None])


def solution(mesh):
    in_specs = (
        P("pipe", "ctx", None),
        P("pipe", "ctx", None),
        P("pipe", "ctx", None),
        P("pipe", "ctx", None),
        P("pipe", None),
        P("pipe", None),
        P("pipe", None),
        P("pipe", None, None),
        P("pipe", None, None),
        P("pipe", None),
        P("pipe", "ctx"),
        P("pipe", "ctx", None),
        P("pipe", "ctx", None),
        P("pipe", "ctx", None),
    )
    out_specs = (P("pipe", "ctx", None), P("pipe", "ctx", None))
    return jax.shard_map(
        on_device, mesh=mesh, in_specs=in_specs, out_specs=out_specs, check_vma=False
    )
```

profile of v0, /device:TPU:0, one launch (start us, length us, event | category | flops | bytes accessed | tf_op | source)
XLA Modules:
  0.0 315.3 jit_solution(9040418585861244815)
XLA Ops:
  2.2 6.3 %all-to-all-start = ((bf16[8,2,512]{2,1,0:T(2,128)(2,1)}), bf16[8,2,512]{2,1,0:T(2,128)(2,1)S(1)}, u32[]{:S(2)}, u32[]{:S(2)}) async-start(bf16[8,2,512]{2,1,0:T(2,128)(2,1)} %reshape.218), calls=%async_computation | async-start | bytes 32768 | tf_op jit(solution)/shard_map/all_to_all | solution.py:129
  8.5 4.3 %reshape_squeeze.16 = bf16[64,128,64]{2,1,0:T(8,128)(2,1)} reshape(bf16[1,64,8192]{2,1,0:T(8,128)(2,1)} %param.16) | data formatting | bytes 2097152 | tf_op jit(solution)/shard_map/reshape;squeeze | solution.py:125
  12.7 3.0 copy.144
  18.4 5.1 %all-to-all-start.1 = ((bf16[8,2,32768]{2,1,0:T(2,128)(2,1)}), bf16[8,2,32768]{2,1,0:T(2,128)(2,1)S(1)}, u32[]{:S(2)}, u32[]{:S(2)}) async-start(bf16[8,2,32768]{2,1,0:T(2,128)(2,1)} %reshape.220), calls=%async_computation.1 | async-start | bytes 2097152 | tf_op jit(solution)/shard_map/all_to_all | solution.py:128
  23.7 6.1 %broadcast_in_dim.176 = bf16[64,4,32,2,128]{4,3,0,2,1:T(2,128)(2,1)} broadcast(bf16[64,4,2,128]{3,2,0,1:T(2,128)(2,1)S(1)} %copy.94), dimensions={0,1,3,4} | broadcast | bytes 4325376 | tf_op jit(solution)/shard_map/broadcast_in_dim | solution.py:42
  29.8 7.6 %reshape_reshape.7 = bf16[64,128,256]{2,0,1:T(8,128)(2,1)} reshape(bf16[64,4,32,2,128]{4,3,0,2,1:T(2,128)(2,1)} %broadcast_in_dim.176) | data formatting | bytes 8388608 | tf_op jit(solution)/shard_map/reshape;reshape | solution.py:43
  37.5 12.6 %all-to-all-done.1 = bf16[8,2,32768]{2,1,0:T(2,128)(2,1)S(1)} async-done(((bf16[8,2,32768]{2,1,0:T(2,128)(2,1)}), bf16[8,2,32768]{2,1,0:T(2,128)(2,1)S(1)}, u32[]{:S(2)}, u32[]{:S(2)}) %all-to-all-start.1) | async-done | bytes 1048608 | tf_op jit(solution)/shard_map/all_to_all | solution.py:128
  50.1 4.6 %all-to-all-start.2 = ((bf16[64,128,256]{2,0,1:T(8,128)(2,1)}), bf16[64,128,256]{2,0,1:T(8,128)(2,1)}, u32[]{:S(2)}, u32[]{:S(2)}) async-start(bf16[64,128,256]{2,0,1:T(8,128)(2,1)} %reshape_reshape.7), calls=%async_computation.2 | async-start | bytes 8388608 | tf_op jit(solution)/shard_map/all_to_all | solution.py:130
  56.6 92.2 %all-reduce.3 = s32[512]{0:T(512)S(1)} all-reduce(s32[512]{0:T(512)S(1)} %bitcast_dynamic-update-slice_fusion), channel_id=2, replica_groups=mesh['pipe'=4,'ctx'=8] {'ctx'}, use_global_device_ids=true, to_apply=%add.3 | all-reduce | flops 512 | bytes 4096 | tf_op jit(solution)/shard_map/all_gather | solution.py:122
  148.8 14.2 %all-gather.1 = bf16[1,512,256]{2,1,0:T(8,128)(2,1)S(1)} all-gather(bf16[1,64,256]{2,1,0:T(8,128)(2,1)S(1)} %copy-done.11), channel_id=3, replica_groups=mesh['pipe'=4,'ctx'=8] {'ctx'}, dimensions={1}, use_global_device_ids=true | all-gather | bytes 294912 | tf_op jit(solution)/shard_map/all_gather | solution.py:170
  167.4 3.1 reshape.221
  170.5 2.9 copy.92
  173.5 3.2 %all_to_all.48 = bf16[512,16,64]{0,2,1:T(8,128)(2,1)S(1)} reshape(bf16[8,64,16,64]{1,0,3,2:T(8,128)(2,1)} %bitcast.252) | data formatting | bytes 2097152 | tf_op jit(solution)/shard_map/all_to_all | solution.py:128
  180.2 4.7 %copy.96 = bf16[8,64,16,256]{3,2,1,0:T(8,128)(2,1)S(1)} copy(bf16[8,64,16,256]{3,1,2,0:T(8,128)(2,1)} %bitcast.17) | data formatting | bytes 8388608 | tf_op jit(solution)/shard_map/all_to_all | solution.py:130
  184.9 7.8 %multiply_convert_fusion = bf16[512,16,256]{2,1,0:T(8,128)(2,1)} fusion(bf16[512,16,256]{2,1,0:T(8,128)(2,1)S(1)} %bitcast.248, f32[16,256]{1,0:T(8,128)S(1)} %get-tuple-element.192, f32[16,256]{1,0:T(8,128)S(1)} %get-tuple-element.190, f32[16,256]{1,0:T(8,128)S(1)} %get-tuple-element.191, f32[16,256]{1,0:T(8,128)S(1)} %get-tuple-element.189, ...), kind=kLoop, calls=%fused_computation.49 | loop fusion | flops 39845888 | bytes 8455680 | tf_op jit(solution)/shard_map/convert_element_type | solution.py:34
  192.7 31.1 %while.3 = (s32[]{:T(128)}, f32[16,64,128]{2,1,0:T(8,128)S(1)}, s32[]{:T(128)}, bf16[2,256,16,64]{1,3,2,0:T(8,128)(2,1)}, s32[2,256]{1,0:T(2,128)S(1)}, /*index=...) while((s32[]{:T(128)}, f32[16,64,128]{2,1,0:T(8,128)S(1)}, ...), condition=%wide.region_3.4_spmd.clone, body=%wide.region_0.3_spmd.clone.sunk | while | flops 882074176 | bytes 19326392 | solution.py:94
  197.0 3.6 %fusion.87 = f32[256,16,64]{0,2,1:T(8,128)} fusion(f32[256,16]{0,1:T(8,128)S(1)} %bitcast.258, f32[256,16]{0,1:T(8,128)S(1)} %bitcast_bitcast_fusion.2, pred[256,256]{0,1:T(8,128)(4,1)S(1)} %fusion.86, bf16[256,16,256]{2,0,1:T(8,128)(2,1)S(1)} %bitcast.242, bf16[2,256,16,64]{1,3,2,0:T(8,128)(2,1)} %get-tuple-element.310, s32[]{:T(128)} %get-tuple-element.289), kind=kOutput, calls=%fused_computation.5.clone.1 | convolution fusion | flops 408944640 | bytes 3785216 | tf_op jit(solution)/shard_map/while/body/eval_jaxpr/tsh,shp->thp/dot_general | solution.py:67
  202.2 3.4 %fusion.88 = bf16[2,256,16,64]{1,3,2,0:T(8,128)(2,1)} fusion(bf16[2,256,16,64]{1,3,2,0:T(8,128)(2,1)} %get-tuple-element.292, s32[]{:T(128)} %get-tuple-element.289, f32[256,16,64]{0,2,1:T(8,128)} %fusion.87, bf16[256,16,256]{2,0,1:T(8,128)(2,1)S(1)} %bitcast.243, f32[16]{0:T(128)S(1)} %get-tuple-element.312, f32[256,16]{0,1:T(8,128)S(1)} %get-tuple-element.274, ...), kind=kOutput, calls=%fused_computation.11.clone.1 | convolution fusion | flops 404094976 | bytes 4211713 | tf_op jit(solution)/shard_map/while/body/eval_jaxpr/thn,hpn->thp/dot_general | solution.py:70
  212.6 3.6 %fusion.87 = f32[256,16,64]{0,2,1:T(8,128)} fusion(f32[256,16]{0,1:T(8,128)S(1)} %bitcast.258, f32[256,16]{0,1:T(8,128)S(1)} %bitcast_bitcast_fusion.2, pred[256,256]{0,1:T(8,128)(4,1)S(1)} %fusion.86, bf16[256,16,256]{2,0,1:T(8,128)(2,1)S(1)} %bitcast.242, bf16[2,256,16,64]{1,3,2,0:T(8,128)(2,1)} %get-tuple-element.310, s32[]{:T(128)} %get-tuple-element.289), kind=kOutput, calls=%fused_computation.5.clone.1 | convolution fusion | flops 408944640 | bytes 3785216 | tf_op jit(solution)/shard_map/while/body/eval_jaxpr/tsh,shp->thp/dot_general | solution.py:67
  217.8 3.4 %fusion.88 = bf16[2,256,16,64]{1,3,2,0:T(8,128)(2,1)} fusion(bf16[2,256,16,64]{1,3,2,0:T(8,128)(2,1)} %get-tuple-element.292, s32[]{:T(128)} %get-tuple-element.289, f32[256,16,64]{0,2,1:T(8,128)} %fusion.87, bf16[256,16,256]{2,0,1:T(8,128)(2,1)S(1)} %bitcast.243, f32[16]{0:T(128)S(1)} %get-tuple-element.312, f32[256,16]{0,1:T(8,128)S(1)} %get-tuple-element.274, ...), kind=kOutput, calls=%fused_computation.11.clone.1 | convolution fusion | flops 404094976 | bytes 4211713 | tf_op jit(solution)/shard_map/while/body/eval_jaxpr/thn,hpn->thp/dot_general | solution.py:70
  223.8 3.0 copy.115
  229.5 4.6 %all-to-all-start.3 = ((bf16[8,2,32768]{2,1,0:T(2,128)(2,1)}), bf16[8,2,32768]{2,1,0:T(2,128)(2,1)}, u32[]{:S(2)}, u32[]{:S(2)}) async-start(bf16[8,2,32768]{2,1,0:T(2,128)(2,1)} %reshape.222), calls=%async_computation.3 | async-start | bytes 2097152 | tf_op jit(solution)/shard_map/all_to_all | solution.py:151
  236.8 30.7 %all-gather.2 = bf16[1,512,256]{2,1,0:T(8,128)(2,1)S(1)} all-gather(bf16[1,64,256]{2,1,0:T(8,128)(2,1)S(1)} %copy-done.12), channel_id=4, replica_groups=mesh['pipe'=4,'ctx'=8] {'ctx'}, dimensions={1}, use_global_device_ids=true | all-gather | bytes 294912 | tf_op jit(solution)/shard_map/all_gather | solution.py:171
  267.7 3.6 %fusion.32 = f32[4,8,64]{2,1,0:T(8,128)S(1)} fusion(f32[4,512,64,8]{1,2,3,0:T(8,128)} %get-tuple-element.203, f32[4,8,64]{2,1,0:T(8,128)S(1)} %get-tuple-element.198, pred[64,512]{1,0:T(8,128)(4,1)S(1)} %copy-done.3), kind=kLoop, calls=%fused_computation.55 | loop fusion | flops 5240832 | bytes 4243456 | tf_op jit(solution)/shard_map/while/body/eval_jaxpr/reduce_sum | solution.py:192
  275.1 3.2 %reshape.196 = f32[64,8,16,64]{3,2,1,0:T(8,128)} reshape(bf16[1,64,8192]{2,1,0:T(8,128)(2,1)S(1)} %copy-done.2) | data formatting | bytes 3145728 | tf_op jit(solution)/shard_map/convert_element_type | solution.py:154
  278.3 5.5 %copy.105 = f32[64,8,16,64]{0,1,3,2:T(8,128)} copy(f32[64,8,16,64]{3,2,1,0:T(8,128)} %reshape.196) | data formatting | bytes 4194304 | tf_op jit(solution)/shard_map/convert_element_type | solution.py:154
  283.8 3.1 reshape.223
  289.4 4.0 %reshape.198 = f32[8,64,16,64]{1,0,3,2:T(8,128)} reshape(bf16[512,16,64]{0,2,1:T(8,128)(2,1)} %copy.102) | data formatting | bytes 3145728 | tf_op jit(solution)/shard_map/convert_element_type | solution.py:154
  293.4 4.9 %multiply_reduce_fusion = f32[64,8]{0,1:T(8,128)S(1)} fusion(f32[64,8,16,64]{0,1,3,2:T(8,128)} %copy.105, f32[8,64,16,64]{1,0,3,2:T(8,128)} %reshape.198), kind=kLoop, calls=%fused_computation.52 | loop fusion | flops 3669504 | bytes 4196352 | tf_op jit(solution)/shard_map/reduce_sum | solution.py:156
  301.2 6.3 %copy.103 = f32[64,8,16,64]{3,2,1,0:T(8,128)} copy(f32[64,8,16,64]{0,1,3,2:T(8,128)} %bitcast.246) | data formatting | bytes 4194304 | tf_op jit(solution)/shard_map/convert_element_type | solution.py:154
  307.5 3.5 %reshape.195 = f32[1,64,8192]{2,1,0:T(8,128)S(1)} reshape(f32[64,8,16,64]{3,2,1,0:T(8,128)} %copy.103) | data formatting | bytes 4194304 | tf_op jit(solution)/shard_map/convert_element_type | solution.py:154
  311.1 3.5 %multiply_convert_fusion.1 = bf16[1,64,8192]{2,1,0:T(8,128)(2,1)} fusion(f32[1,64,8192]{2,1,0:T(8,128)} %mul.292, f32[1,64,8192]{2,1,0:T(8,128)S(1)} %reshape.195, f32[8192]{0:T(1024)S(1)} %bitcast.262, bf16[1,64,8192]{2,1,0:T(8,128)(2,1)} %param.17), kind=kLoop, calls=%fused_computation.57 | loop fusion | flops 4718592 | bytes 6324224 | tf_op jit(solution)/shard_map/convert_element_type | solution.py:159
  (138 shorter events, 43.3 us)
Async XLA Ops:
  2.2 16.2 %all-to-all-start = ((bf16[8,2,512]{2,1,0:T(2,128)(2,1)}), bf16[8,2,512]{2,1,0:T(2,128)(2,1)S(1)}, u32[]{:S(2)}, u32[]{:S(2)}) async-start(bf16[8,2,512]{2,1,0:T(2,128)(2,1)} %reshape.218), calls=%async_computation | async-start | bytes 32768 | tf_op jit(solution)/shard_map/all_to_all | solution.py:129
  12.7 10.7 %copy-start.5 = (bf16[1,64,1024]{2,1,0:T(8,128)(2,1)S(1)}, bf16[1,64,1024]{2,1,0:T(8,128)(2,1)}, u32[]{:S(2)}) copy-start(bf16[1,64,1024]{2,1,0:T(8,128)(2,1)} %param.18) | copy-start | bytes 393220
  18.4 31.7 %all-to-all-start.1 = ((bf16[8,2,32768]{2,1,0:T(2,128)(2,1)}), bf16[8,2,32768]{2,1,0:T(2,128)(2,1)S(1)}, u32[]{:S(2)}, u32[]{:S(2)}) async-start(bf16[8,2,32768]{2,1,0:T(2,128)(2,1)} %reshape.220), calls=%async_computation.1 | async-start | bytes 2097152 | tf_op jit(solution)/shard_map/all_to_all | solution.py:128
  37.4 17.3 %copy-start.15 = (bf16[1,4,1024]{2,1,0:T(4,128)(2,1)S(1)}, bf16[1,4,1024]{2,1,0:T(4,128)(2,1)}, u32[]{:S(2)}) copy-start(bf16[1,4,1024]{2,1,0:T(4,128)(2,1)} %param.24) | copy-start | bytes 24580
  37.4 17.7 %copy-start.6 = (bf16[1,4,8192]{2,1,0:T(4,128)(2,1)S(1)}, bf16[1,4,8192]{2,1,0:T(4,128)(2,1)}, u32[]{:S(2)}) copy-start(bf16[1,4,8192]{2,1,0:T(4,128)(2,1)} %param.23) | copy-start | bytes 196612
  37.4 17.8 %copy-start.23 = (u32[32]{0:T(128)S(1)}, u32[32]{0:T(128)}, u32[]{:S(2)}) copy-start(u32[32]{0:T(128)} %constant.111) | copy-start | bytes 388
  37.4 19.1 %copy-start.19 = (s32[1,64]{1,0:T(1,128)S(1)}, s32[1,64]{1,0:T(1,128)}, u32[]{:S(2)}) copy-start(s32[1,64]{1,0:T(1,128)} %param.26) | copy-start | bytes 772
  37.4 111.4 %copy-start.11 = (bf16[1,64,256]{2,1,0:T(8,128)(2,1)S(1)}, bf16[1,64,256]{2,1,0:T(8,128)(2,1)}, u32[]{:S(2)}) copy-start(bf16[1,64,256]{2,1,0:T(8,128)(2,1)} %param.28) | copy-start | bytes 98308
  37.4 125.7 %copy-start.4 = (bf16[1,64,2048]{2,1,0:T(8,128)(2,1)S(1)}, bf16[1,64,2048]{2,1,0:T(8,128)(2,1)}, u32[]{:S(2)}) copy-start(bf16[1,64,2048]{2,1,0:T(8,128)(2,1)} %param.27) | copy-start | bytes 786436
  37.4 126.2 %copy-start.22 = (f32[1,128]{1,0:T(1,128)S(1)}, f32[1,128]{1,0:T(1,128)}, u32[]{:S(2)}) copy-start(f32[1,128]{1,0:T(1,128)} %param.20) | copy-start | bytes 1540
  37.5 126.8 %copy-start.20 = (f32[1,128]{1,0:T(1,128)S(1)}, f32[1,128]{1,0:T(1,128)}, u32[]{:S(2)}) copy-start(f32[1,128]{1,0:T(1,128)} %param.21) | copy-start | bytes 1540
  37.5 126.8 %copy-start.21 = (f32[1,128]{1,0:T(1,128)S(1)}, f32[1,128]{1,0:T(1,128)}, u32[]{:S(2)}) copy-start(f32[1,128]{1,0:T(1,128)} %param.22) | copy-start | bytes 1540
  50.1 4.6 %copy-start.1 = (bf16[8,2,32768]{2,1,0:T(2,128)(2,1)}, bf16[8,2,32768]{2,1,0:T(2,128)(2,1)S(1)}, u32[]{:S(2)}) copy-start(bf16[8,2,32768]{2,1,0:T(2,128)(2,1)S(1)} %all-to-all-done.1) | copy-start | bytes 3145732
  50.1 130.1 %all-to-all-start.2 = ((bf16[64,128,256]{2,0,1:T(8,128)(2,1)}), bf16[64,128,256]{2,0,1:T(8,128)(2,1)}, u32[]{:S(2)}, u32[]{:S(2)}) async-start(bf16[64,128,256]{2,0,1:T(8,128)(2,1)} %reshape_reshape.7), calls=%async_computation.2 | async-start | bytes 8388608 | tf_op jit(solution)/shard_map/all_to_all | solution.py:130
  170.5 6.2 %copy-start.8 = (f32[16,64]{1,0:T(8,128)S(1)}, f32[16,64]{1,0:T(8,128)}, u32[]{:S(2)}) copy-start(f32[16,64]{1,0:T(8,128)} %get-tuple-element.194) | copy-start | bytes 12292
  170.5 6.2 %copy-start.9 = (f32[16,64]{1,0:T(8,128)S(1)}, f32[16,64]{1,0:T(8,128)}, u32[]{:S(2)}) copy-start(f32[16,64]{1,0:T(8,128)} %get-tuple-element.195) | copy-start | bytes 12292
  170.5 6.2 %copy-start.10 = (f32[16,64]{1,0:T(8,128)S(1)}, f32[16,64]{1,0:T(8,128)}, u32[]{:S(2)}) copy-start(f32[16,64]{1,0:T(8,128)} %get-tuple-element.196) | copy-start | bytes 12292
  170.5 6.2 %copy-start.16 = (pred[512]{0:T(512)(128)(4,1)S(1)}, pred[512]{0:T(512)(128)(4,1)}, u32[]{:S(2)}) copy-start(pred[512]{0:T(512)(128)(4,1)} %get-tuple-element.199) | copy-start | bytes 1540
  170.5 6.2 %copy-start.17 = (pred[512]{0:T(512)(128)(4,1)S(1)}, pred[512]{0:T(512)(128)(4,1)}, u32[]{:S(2)}) copy-start(pred[512]{0:T(512)(128)(4,1)} %get-tuple-element.200) | copy-start | bytes 1540
  170.5 6.2 %copy-start.18 = (pred[512]{0:T(512)(128)(4,1)S(1)}, pred[512]{0:T(512)(128)(4,1)}, u32[]{:S(2)}) copy-start(pred[512]{0:T(512)(128)(4,1)} %get-tuple-element.201) | copy-start | bytes 1540
  184.9 7.8 %copy-start.13 = (f32[16]{0:T(128)S(1)}, f32[16]{0:T(128)}, u32[]{:S(2)}) copy-start(f32[16]{0:T(128)} %fusion.63) | copy-start | bytes 196
  200.6 7.0 %copy-start.14 = (f32[16]{0:T(128)S(1)}, f32[16]{0:T(128)}, u32[]{:S(2)}) copy-start(f32[16]{0:T(128)} %get-tuple-element.345) | copy-start | bytes 196 | tf_op jit(solution)/shard_map/while
  216.2 7.0 %copy-start.14 = (f32[16]{0:T(128)S(1)}, f32[16]{0:T(128)}, u32[]{:S(2)}) copy-start(f32[16]{0:T(128)} %get-tuple-element.345) | copy-start | bytes 196 | tf_op jit(solution)/shard_map/while
  223.8 10.3 %copy-start.3 = (pred[64,512]{1,0:T(8,128)(4,1)S(1)}, pred[64,512]{1,0:T(8,128)(4,1)}, u32[]{:S(2)}) copy-start(pred[64,512]{1,0:T(8,128)(4,1)} %fusion.47) | copy-start | bytes 98308
  229.5 7.3 %copy-start.12 = (bf16[1,64,256]{2,1,0:T(8,128)(2,1)S(1)}, bf16[1,64,256]{2,1,0:T(8,128)(2,1)}, u32[]{:S(2)}) copy-start(bf16[1,64,256]{2,1,0:T(8,128)(2,1)} %param.29) | copy-start | bytes 98308
  229.5 54.3 %all-to-all-start.3 = ((bf16[8,2,32768]{2,1,0:T(2,128)(2,1)}), bf16[8,2,32768]{2,1,0:T(2,128)(2,1)}, u32[]{:S(2)}, u32[]{:S(2)}) async-start(bf16[8,2,32768]{2,1,0:T(2,128)(2,1)} %reshape.222), calls=%async_computation.3 | async-start | bytes 2097152 | tf_op jit(solution)/shard_map/all_to_all | solution.py:151
  267.6 3.6 %copy-start = (f32[4,512,64,8]{1,2,3,0:T(8,128)S(1)}, f32[4,512,64,8]{1,2,3,0:T(8,128)}, u32[]{:S(2)}) copy-start(f32[4,512,64,8]{1,2,3,0:T(8,128)} %get-tuple-element.203) | copy-start | bytes 12582916
  271.3 3.8 %copy-start.2 = (bf16[1,64,8192]{2,1,0:T(8,128)(2,1)S(1)}, bf16[1,64,8192]{2,1,0:T(8,128)(2,1)}, u32[]{:S(2)}) copy-start(bf16[1,64,8192]{2,1,0:T(8,128)(2,1)} %param.17) | copy-start | bytes 3145732
  273.5 10.3 %collective-permute-start = (bf16[64,2048]{1,0:T(8,128)(2,1)S(1)}, bf16[64,2048]{1,0:T(8,128)(2,1)S(1)}, u32[]{:S(2)}, u32[]{:S(2)}) collective-permute-start(bf16[64,2048]{1,0:T(8,128)(2,1)S(1)} %convert_element_type.151), channel_id=1, source_target_pairs={{0,8},{8,16},{16,24},{24,0},{1,9},{9,17},{17,25},{25,1},{2,10},{10... | collective-permute-start | bytes 786440 | tf_op jit(solution)/shard_map/ppermute | solution.py:17
  307.5 3.5 %copy-start.7 = (f32[1,8192]{1,0:T(1,128)S(1)}, f32[1,8192]{1,0:T(1,128)}, u32[]{:S(2)}) copy-start(f32[1,8192]{1,0:T(1,128)} %param.25) | copy-start | bytes 98308
where the time goes:
time: 317 us; the launch traced here: 315 us
  blocking collectives  137 us (43%)
  local copies, waits for them, and re-layouts  89.4 us (28%)
  other arithmetic  28.6 us (9%)
  starting transfers between devices  22.1 us (7%)
  matrix products  21.1 us (7%)
  waiting for transfers between devices  12.6 us (4%)
    all_gather x1, blocking collectives, on_device(): all_ids = lax.all_gather(own_ids, 'ctx', axis=0, tiled=True)  92.2 us
    all_gather x1, blocking collectives, on_device(): value_piece = lax.all_gather(values[0], 'ctx', axis=0, tiled=True)  30.7 us
    unnamed x57, local copies, waits for them, and re-layouts  14.6 us
    all_gather x1, blocking collectives, on_device(): key_piece = lax.all_gather(keys[0], 'ctx', axis=0, tiled=True)  14.2 us
    convert_element_type x3, local copies, waits for them, and re-layouts, on_device(): mixed_tokens.astype(jnp.float32) * jax.nn.silu(z_in[0].astype(jnp.float32))  13.9 us
    all_to_all x1, waiting for transfers between devices, on_device(): lax.all_to_all(x_send, 'ctx', split_axis=1, concat_axis=0, tiled=True)  12.6 us
    convert_element_type x2, other arithmetic, causal_taps(): return jax.nn.silu(summed).astype(jnp.bfloat16)  10 us
    convert_element_type x2, local copies, waits for them, and re-layouts, on_device(): z_in[0].astype(jnp.float32)  8.7 us
  transfers between devices with their start and end apart: 5, of which 1 were waited for; matrix products, arithmetic and copies ran while one was open for 18% of the time, Pallas kernels for 0%

commit v1 on v0

--- a/solution.py
+++ b/solution.py
@@ -9,6 +9,29 @@
 KVH = 4
 HD = 64
 norm_eps = 1e-05
+
+
+def in_order(blocks, dim):
+    blocks = jnp.moveaxis(blocks, 0, dim)
+    shape = blocks.shape
+    return blocks.reshape(*shape[:dim], shape[dim] * shape[dim + 1], *shape[dim + 2 :])
+
+
+def doubled(array, axis):
+    devices, index = (lax.axis_size(axis), lax.axis_index(axis))
+    blocks, distance = (array[None], 1)
+    while distance < devices:
+        partner_block = lax.ppermute(blocks, axis, [(i, i ^ distance) for i in range(devices)])
+        low = index & distance == 0
+        blocks = jnp.concatenate(
+            [jnp.where(low, blocks, partner_block), jnp.where(low, partner_block, blocks)]
+        )
+        distance *= 2
+    return blocks
+
+
+def doubled_up(x, axis, dim):
+    return in_order(doubled(x, axis), dim)
 
 
 def from_behind(value, axis, steps):
@@ -167,7 +190,7 @@
         jnp.zeros((KVH, ratio, tokens_here, HD), jnp.float32),
     )
     carry = initial
-    key_piece = lax.all_gather(keys[0], "ctx", axis=0, tiled=True)
+    key_piece = doubled_up(keys[0], "ctx", 0)
     value_piece = lax.all_gather(values[0], "ctx", axis=0, tiled=True)
     count = key_piece.shape[0]
     width = math.gcd(count, 512)

time: 317 us -> 298 us (0.940)
  blocking collectives: 137 us -> 106 us
  waiting for transfers between devices: 12.6 us -> 35 us
  other arithmetic: 28.6 us -> 23.2 us
  local copies, waits for them, and re-layouts: 89.4 us -> 85.6 us
    all_gather x1, blocking collectives: 30.7 us -> 14.2 us  [on_device(): value_piece = lax.all_gather(values[0], 'ctx', axis=0, tiled=True)]
    all_gather x1 -> x0, blocking collectives: 14.2 us -> none  [on_device(): key_piece = lax.all_gather(keys[0], 'ctx', axis=0, tiled=True)]
    ppermute x0 -> x3, waiting for transfers between devices: none -> 12.1 us  [doubled(): lax.ppermute(blocks, axis, [(i, i ^ distance) for i in range(devices)])]
    all_to_all x1, waiting for transfers between devices: 0.01 us -> 10.3 us  [on_device(): lax.all_to_all(attention_mixture, 'ctx', split_axis=0, concat_axis=1, til...]
    unnamed x57 -> x41, local copies, waits for them, and re-layouts: 14.6 us -> 12.9 us
  transfers between devices with their start and end apart: 5 -> 8, of which waited for: 1 -> 4; matrix products, arithmetic and copies ran while one was open for 18% -> 18% of each run, Pallas kernels for 0% -> 0%
where the time goes in v1:
time: 298 us; the launch traced here: 297 us
  blocking collectives  106 us (36%)
  local copies, waits for them, and re-layouts  85.6 us (29%)
  waiting for transfers between devices  35 us (12%)
  other arithmetic  23.2 us (8%)
  starting transfers between devices  22.4 us (8%)
  matrix products  20.4 us (7%)
    all_gather x1, blocking collectives, on_device(): all_ids = lax.all_gather(own_ids, 'ctx', axis=0, tiled=True)  91.9 us
    all_gather x1, blocking collectives, on_device(): value_piece = lax.all_gather(values[0], 'ctx', axis=0, tiled=True)  14.2 us
    unnamed x41, local copies, waits for them, and re-layouts  12.9 us
    all_to_all x1, waiting for transfers between devices, on_device(): lax.all_to_all(x_send, 'ctx', split_axis=1, concat_axis=0, tiled=True)  12.6 us
    convert_element_type x3, local copies, waits for them, and re-layouts, on_device(): mixed_tokens.astype(jnp.float32) * jax.nn.silu(z_in[0].astype(jnp.float32))  12.3 us
    ppermute x3, waiting for transfers between devices, doubled(): lax.ppermute(blocks, axis, [(i, i ^ distance) for i in range(devices)])  12.1 us
    all_to_all x1, waiting for transfers between devices, on_device(): lax.all_to_all(attention_mixture, 'ctx', split_axis=0, concat_axis=1, til...  10.3 us
    convert_element_type x2, other arithmetic, causal_taps(): return jax.nn.silu(summed).astype(jnp.bfloat16)  10 us
  transfers between devices with their start and end apart: 8, of which 4 were waited for; matrix products, arithmetic and copies ran while one was open for 18% of the time, Pallas kernels for 0%

profile of v1, /device:TPU:0, one launch (start us, length us, event | category | flops | bytes accessed | tf_op | source)
XLA Modules:
  0.0 297.1 jit_solution(4981214089558017275)
XLA Ops:
  2.2 6.3 %all-to-all-start = ((bf16[8,2,512]{2,1,0:T(2,128)(2,1)}), bf16[8,2,512]{2,1,0:T(2,128)(2,1)S(1)}, u32[]{:S(2)}, u32[]{:S(2)}) async-start(bf16[8,2,512]{2,1,0:T(2,128)(2,1)} %reshape.216), calls=%async_computation | async-start | bytes 32768 | tf_op jit(solution)/shard_map/all_to_all | solution.py:152
  8.5 4.2 %reshape_squeeze.16 = bf16[64,128,64]{2,1,0:T(8,128)(2,1)} reshape(bf16[1,64,8192]{2,1,0:T(8,128)(2,1)} %param.16) | data formatting | bytes 2097152 | tf_op jit(solution)/shard_map/reshape;squeeze | solution.py:148
  12.7 3.0 %copy.151 = bf16[64,128,64]{2,0,1:T(8,128)(2,1)S(1)} copy(bf16[64,128,64]{2,1,0:T(8,128)(2,1)} %reshape_squeeze.16) | data formatting | bytes 2097152 | tf_op jit(solution)/shard_map/reshape;squeeze | solution.py:148
  15.7 2.7 reshape.218
  18.4 5.1 %all-to-all-start.1 = ((bf16[8,2,32768]{2,1,0:T(2,128)(2,1)}), bf16[8,2,32768]{2,1,0:T(2,128)(2,1)S(1)}, u32[]{:S(2)}, u32[]{:S(2)}) async-start(bf16[8,2,32768]{2,1,0:T(2,128)(2,1)} %reshape.218), calls=%async_computation.1 | async-start | bytes 2097152 | tf_op jit(solution)/shard_map/all_to_all | solution.py:151
  23.7 6.1 %broadcast_in_dim.176 = bf16[64,4,32,2,128]{4,3,0,2,1:T(2,128)(2,1)} broadcast(bf16[64,4,2,128]{3,2,0,1:T(2,128)(2,1)S(1)} %copy.94), dimensions={0,1,3,4} | broadcast | bytes 4325376 | tf_op jit(solution)/shard_map/broadcast_in_dim | solution.py:65
  29.8 7.6 %reshape_reshape.8 = bf16[64,128,256]{2,0,1:T(8,128)(2,1)} reshape(bf16[64,4,32,2,128]{4,3,0,2,1:T(2,128)(2,1)} %broadcast_in_dim.176) | data formatting | bytes 8388608 | tf_op jit(solution)/shard_map/reshape;reshape | solution.py:66
  37.5 12.6 %all-to-all-done.1 = bf16[8,2,32768]{2,1,0:T(2,128)(2,1)S(1)} async-done(((bf16[8,2,32768]{2,1,0:T(2,128)(2,1)}), bf16[8,2,32768]{2,1,0:T(2,128)(2,1)S(1)}, u32[]{:S(2)}, u32[]{:S(2)}) %all-to-all-start.1) | async-done | bytes 1048608 | tf_op jit(solution)/shard_map/all_to_all | solution.py:151
  50.1 4.6 %all-to-all-start.2 = ((bf16[64,128,256]{2,0,1:T(8,128)(2,1)}), bf16[64,128,256]{2,0,1:T(8,128)(2,1)}, u32[]{:S(2)}, u32[]{:S(2)}) async-start(bf16[64,128,256]{2,0,1:T(8,128)(2,1)} %reshape_reshape.8), calls=%async_computation.2 | async-start | bytes 8388608 | tf_op jit(solution)/shard_map/all_to_all | solution.py:153
  56.9 91.9 %all-reduce.3 = s32[512]{0:T(512)S(1)} all-reduce(s32[512]{0:T(512)S(1)} %bitcast_dynamic-update-slice_fusion), channel_id=2, replica_groups=mesh['pipe'=4,'ctx'=8] {'ctx'}, use_global_device_ids=true, to_apply=%add.3 | all-reduce | flops 512 | bytes 4096 | tf_op jit(solution)/shard_map/all_gather | solution.py:145
  148.9 14.2 %all-gather.1 = bf16[1,512,256]{2,1,0:T(8,128)(2,1)S(1)} all-gather(bf16[1,64,256]{2,1,0:T(8,128)(2,1)S(1)} %copy-done.7), channel_id=3, replica_groups=mesh['pipe'=4,'ctx'=8] {'ctx'}, dimensions={1}, use_global_device_ids=true | all-gather | bytes 294912 | tf_op jit(solution)/shard_map/all_gather | solution.py:194
  165.2 4.2 %collective-permute-done.1 = bf16[2,64,256]{2,1,0:T(8,128)(2,1)S(1)} collective-permute-done((bf16[2,64,256]{2,1,0:T(8,128)(2,1)S(1)}, bf16[2,64,256]{2,1,0:T(8,128)(2,1)S(1)}, u32[]{:S(2)}, u32[]{:S(2)}) %collective-permute-start.1) | collective-permute-done | bytes 65568 | tf_op jit(solution)/shard_map/ppermute | solution.py:24
  170.3 7.9 %collective-permute-done.2 = bf16[4,64,256]{2,1,0:T(8,128)(2,1)S(1)} collective-permute-done((bf16[4,64,256]{2,1,0:T(8,128)(2,1)S(1)}, bf16[4,64,256]{2,1,0:T(8,128)(2,1)S(1)}, u32[]{:S(2)}, u32[]{:S(2)}) %collective-permute-start.2) | collective-permute-done | bytes 131104 | tf_op jit(solution)/shard_map/ppermute | solution.py:24
  179.3 3.1 %reshape.219 = bf16[128,64,64]{2,1,0:T(8,128)(2,1)S(1)} reshape(bf16[8,2,32768]{2,1,0:T(2,128)(2,1)} %copy-done) | data formatting | bytes 2097152
  182.4 2.9 copy.92
  185.3 3.2 %all_to_all.48 = bf16[512,16,64]{0,2,1:T(8,128)(2,1)S(1)} reshape(bf16[8,64,16,64]{1,0,3,2:T(8,128)(2,1)} %bitcast.247) | data formatting | bytes 2097152 | tf_op jit(solution)/shard_map/all_to_all | solution.py:151
  191.9 4.7 %copy.96 = bf16[8,64,16,256]{3,2,1,0:T(8,128)(2,1)S(1)} copy(bf16[8,64,16,256]{3,1,2,0:T(8,128)(2,1)} %bitcast.17) | data formatting | bytes 8388608 | tf_op jit(solution)/shard_map/all_to_all | solution.py:153
  196.7 7.8 %multiply_convert_fusion = bf16[512,16,256]{2,1,0:T(8,128)(2,1)} fusion(bf16[512,16,256]{2,1,0:T(8,128)(2,1)S(1)} %bitcast.243, f32[16,256]{1,0:T(8,128)S(1)} %get-tuple-element.194, f32[16,256]{1,0:T(8,128)S(1)} %get-tuple-element.192, f32[16,256]{1,0:T(8,128)S(1)} %get-tuple-element.193, f32[16,256]{1,0:T(8,128)S(1)} %get-tuple-element.191, ...), kind=kLoop, calls=%fused_computation.49 | loop fusion | flops 39845888 | bytes 8455680 | tf_op jit(solution)/shard_map/convert_element_type | solution.py:57
  204.5 29.6 %while.3 = (s32[]{:T(128)}, f32[16,64,128]{2,1,0:T(8,128)S(1)}, s32[]{:T(128)}, bf16[2,256,16,64]{1,3,2,0:T(8,128)(2,1)}, s32[2,256]{1,0:T(2,128)S(1)}, /*index=...) while((s32[]{:T(128)}, f32[16,64,128]{2,1,0:T(8,128)S(1)}, ...), condition=%wide.region_3.4_spmd.clone, body=%wide.region_0.3_spmd.clone.sunk | while | flops 882074176 | bytes 19326100 | solution.py:117
  208.0 3.6 %fusion.87 = f32[256,16,64]{0,2,1:T(8,128)} fusion(f32[256,16]{0,1:T(8,128)S(1)} %bitcast.253, f32[256,16]{0,1:T(8,128)S(1)} %bitcast_bitcast_fusion.2, pred[256,256]{0,1:T(8,128)(4,1)S(1)} %fusion.86, bf16[256,16,256]{2,0,1:T(8,128)(2,1)S(1)} %bitcast.237, bf16[2,256,16,64]{1,3,2,0:T(8,128)(2,1)} %get-tuple-element.316, s32[]{:T(128)} %get-tuple-element.295), kind=kOutput, calls=%fused_computation.5.clone.1 | convolution fusion | flops 408944640 | bytes 3785216 | tf_op jit(solution)/shard_map/while/body/eval_jaxpr/tsh,shp->thp/dot_general | solution.py:90
  213.2 3.4 %fusion.88 = bf16[2,256,16,64]{1,3,2,0:T(8,128)(2,1)} fusion(bf16[2,256,16,64]{1,3,2,0:T(8,128)(2,1)} %get-tuple-element.298, s32[]{:T(128)} %get-tuple-element.295, f32[256,16,64]{0,2,1:T(8,128)} %fusion.87, bf16[256,16,256]{2,0,1:T(8,128)(2,1)S(1)} %bitcast.238, f32[16]{0:T(128)S(1)} %get-tuple-element.318, f32[256,16]{0,1:T(8,128)S(1)} %get-tuple-element.280, ...), kind=kOutput, calls=%fused_computation.11.clone.1 | convolution fusion | flops 404094976 | bytes 4211713 | tf_op jit(solution)/shard_map/while/body/eval_jaxpr/thn,hpn->thp/dot_general | solution.py:93
  222.8 3.6 %fusion.87 = f32[256,16,64]{0,2,1:T(8,128)} fusion(f32[256,16]{0,1:T(8,128)S(1)} %bitcast.253, f32[256,16]{0,1:T(8,128)S(1)} %bitcast_bitcast_fusion.2, pred[256,256]{0,1:T(8,128)(4,1)S(1)} %fusion.86, bf16[256,16,256]{2,0,1:T(8,128)(2,1)S(1)} %bitcast.237, bf16[2,256,16,64]{1,3,2,0:T(8,128)(2,1)} %get-tuple-element.316, s32[]{:T(128)} %get-tuple-element.295), kind=kOutput, calls=%fused_computation.5.clone.1 | convolution fusion | flops 408944640 | bytes 3785216 | tf_op jit(solution)/shard_map/while/body/eval_jaxpr/tsh,shp->thp/dot_general | solution.py:90
  228.0 3.4 %fusion.88 = bf16[2,256,16,64]{1,3,2,0:T(8,128)(2,1)} fusion(bf16[2,256,16,64]{1,3,2,0:T(8,128)(2,1)} %get-tuple-element.298, s32[]{:T(128)} %get-tuple-element.295, f32[256,16,64]{0,2,1:T(8,128)} %fusion.87, bf16[256,16,256]{2,0,1:T(8,128)(2,1)S(1)} %bitcast.238, f32[16]{0:T(128)S(1)} %get-tuple-element.318, f32[256,16]{0,1:T(8,128)S(1)} %get-tuple-element.280, ...), kind=kOutput, calls=%fused_computation.11.clone.1 | convolution fusion | flops 404094976 | bytes 4211713 | tf_op jit(solution)/shard_map/while/body/eval_jaxpr/thn,hpn->thp/dot_general | solution.py:93
  234.1 3.0 %copy.115 = bf16[2,256,16,64]{3,2,1,0:T(8,128)(2,1)S(1)} copy(bf16[2,256,16,64]{1,3,2,0:T(8,128)(2,1)} %get-tuple-element.89) | data formatting | bytes 2097152 | tf_op jit(solution)/shard_map/convert_element_type | solution.py:173
  239.7 3.8 %all-to-all-start.3 = ((bf16[8,2,32768]{2,1,0:T(2,128)(2,1)}), bf16[8,2,32768]{2,1,0:T(2,128)(2,1)S(1)}, u32[]{:S(2)}, u32[]{:S(2)}) async-start(bf16[8,2,32768]{2,1,0:T(2,128)(2,1)} %reshape.220), calls=%async_computation.3 | async-start | bytes 2097152 | tf_op jit(solution)/shard_map/all_to_all | solution.py:174
  250.8 3.2 %reshape.195 = f32[64,8,16,64]{3,2,1,0:T(8,128)} reshape(bf16[1,64,8192]{2,1,0:T(8,128)(2,1)S(1)} %copy-done.1) | data formatting | bytes 3145728 | tf_op jit(solution)/shard_map/convert_element_type | solution.py:177
  254.0 5.5 %copy.105 = f32[64,8,16,64]{0,1,3,2:T(8,128)} copy(f32[64,8,16,64]{3,2,1,0:T(8,128)} %reshape.195) | data formatting | bytes 4194304 | tf_op jit(solution)/shard_map/convert_element_type | solution.py:177
  259.5 10.3 %all-to-all-done.3 = bf16[8,2,32768]{2,1,0:T(2,128)(2,1)S(1)} async-done(((bf16[8,2,32768]{2,1,0:T(2,128)(2,1)}), bf16[8,2,32768]{2,1,0:T(2,128)(2,1)S(1)}, u32[]{:S(2)}, u32[]{:S(2)}) %all-to-all-start.3) | async-done | bytes 1048608 | tf_op jit(solution)/shard_map/all_to_all | solution.py:174
  275.3 4.9 %multiply_reduce_fusion = f32[64,8]{0,1:T(8,128)S(1)} fusion(f32[64,8,16,64]{0,1,3,2:T(8,128)} %copy.105, f32[8,64,16,64]{1,0,3,2:T(8,128)} %reshape.197), kind=kLoop, calls=%fused_computation.52 | loop fusion | flops 3669504 | bytes 4196352 | tf_op jit(solution)/shard_map/reduce_sum | solution.py:179
  283.2 6.3 %copy.103 = f32[64,8,16,64]{3,2,1,0:T(8,128)} copy(f32[64,8,16,64]{0,1,3,2:T(8,128)} %bitcast.241) | data formatting | bytes 4194304 | tf_op jit(solution)/shard_map/convert_element_type | solution.py:177
  289.5 3.6 %reshape.194 = f32[1,64,8192]{2,1,0:T(8,128)S(1)} reshape(f32[64,8,16,64]{3,2,1,0:T(8,128)} %copy.103) | data formatting | bytes 4194304 | tf_op jit(solution)/shard_map/convert_element_type | solution.py:177
  293.1 3.3 %multiply_convert_fusion.1 = bf16[1,64,8192]{2,1,0:T(8,128)(2,1)} fusion(f32[1,64,8192]{2,1,0:T(8,128)} %mul.292, f32[1,64,8192]{2,1,0:T(8,128)S(1)} %reshape.194, f32[8192]{0:T(1024)S(1)} %bitcast.257, bf16[1,64,8192]{2,1,0:T(8,128)(2,1)S(1)} %copy-done.2), kind=kLoop, calls=%fused_computation.57 | loop fusion | flops 4718592 | bytes 6324224 | tf_op jit(solution)/shard_map/convert_element_type | solution.py:182
  (129 shorter events, 42.7 us)
Async XLA Ops:
  2.2 16.2 %all-to-all-start = ((bf16[8,2,512]{2,1,0:T(2,128)(2,1)}), bf16[8,2,512]{2,1,0:T(2,128)(2,1)S(1)}, u32[]{:S(2)}, u32[]{:S(2)}) async-start(bf16[8,2,512]{2,1,0:T(2,128)(2,1)} %reshape.216), calls=%async_computation | async-start | bytes 32768 | tf_op jit(solution)/shard_map/all_to_all | solution.py:152
  12.7 10.7 %copy-start.4 = (bf16[1,64,1024]{2,1,0:T(8,128)(2,1)S(1)}, bf16[1,64,1024]{2,1,0:T(8,128)(2,1)}, u32[]{:S(2)}) copy-start(bf16[1,64,1024]{2,1,0:T(8,128)(2,1)} %param.18) | copy-start | bytes 393220
  18.4 31.7 %all-to-all-start.1 = ((bf16[8,2,32768]{2,1,0:T(2,128)(2,1)}), bf16[8,2,32768]{2,1,0:T(2,128)(2,1)S(1)}, u32[]{:S(2)}, u32[]{:S(2)}) async-start(bf16[8,2,32768]{2,1,0:T(2,128)(2,1)} %reshape.218), calls=%async_computation.1 | async-start | bytes 2097152 | tf_op jit(solution)/shard_map/all_to_all | solution.py:151
  37.4 17.2 %copy-start.8 = (bf16[1,64,256]{2,1,0:T(8,128)(2,1)S(1)}, bf16[1,64,256]{2,1,0:T(8,128)(2,1)}, u32[]{:S(2)}) copy-start(bf16[1,64,256]{2,1,0:T(8,128)(2,1)} %param.28) | copy-start | bytes 98308
  37.4 17.6 %copy-start.9 = (bf16[1,4,1024]{2,1,0:T(4,128)(2,1)S(1)}, bf16[1,4,1024]{2,1,0:T(4,128)(2,1)}, u32[]{:S(2)}) copy-start(bf16[1,4,1024]{2,1,0:T(4,128)(2,1)} %param.24) | copy-start | bytes 24580
  37.4 18.0 %copy-start.5 = (bf16[1,4,8192]{2,1,0:T(4,128)(2,1)S(1)}, bf16[1,4,8192]{2,1,0:T(4,128)(2,1)}, u32[]{:S(2)}) copy-start(bf16[1,4,8192]{2,1,0:T(4,128)(2,1)} %param.23) | copy-start | bytes 196612
  37.4 18.1 %copy-start.14 = (u32[32]{0:T(128)S(1)}, u32[32]{0:T(128)}, u32[]{:S(2)}) copy-start(u32[32]{0:T(128)} %constant.117) | copy-start | bytes 388
  37.4 19.4 %copy-start.10 = (s32[1,64]{1,0:T(1,128)S(1)}, s32[1,64]{1,0:T(1,128)}, u32[]{:S(2)}) copy-start(s32[1,64]{1,0:T(1,128)} %param.26) | copy-start | bytes 772
  37.4 111.4 %copy-start.11 = (f32[1,128]{1,0:T(1,128)S(1)}, f32[1,128]{1,0:T(1,128)}, u32[]{:S(2)}) copy-start(f32[1,128]{1,0:T(1,128)} %param.21) | copy-start | bytes 1540
  37.5 111.3 %copy-start.12 = (f32[1,128]{1,0:T(1,128)S(1)}, f32[1,128]{1,0:T(1,128)}, u32[]{:S(2)}) copy-start(f32[1,128]{1,0:T(1,128)} %param.22) | copy-start | bytes 1540
  37.5 111.4 %copy-start.7 = (bf16[1,64,256]{2,1,0:T(8,128)(2,1)S(1)}, bf16[1,64,256]{2,1,0:T(8,128)(2,1)}, u32[]{:S(2)}) copy-start(bf16[1,64,256]{2,1,0:T(8,128)(2,1)} %param.29) | copy-start | bytes 98308
  37.5 125.8 %copy-start.13 = (f32[1,128]{1,0:T(1,128)S(1)}, f32[1,128]{1,0:T(1,128)}, u32[]{:S(2)}) copy-start(f32[1,128]{1,0:T(1,128)} %param.20) | copy-start | bytes 1540
  37.5 125.9 %copy-start.3 = (bf16[1,64,2048]{2,1,0:T(8,128)(2,1)S(1)}, bf16[1,64,2048]{2,1,0:T(8,128)(2,1)}, u32[]{:S(2)}) copy-start(bf16[1,64,2048]{2,1,0:T(8,128)(2,1)} %param.27) | copy-start | bytes 786436
  50.1 4.9 %copy-start = (bf16[8,2,32768]{2,1,0:T(2,128)(2,1)}, bf16[8,2,32768]{2,1,0:T(2,128)(2,1)S(1)}, u32[]{:S(2)}) copy-start(bf16[8,2,32768]{2,1,0:T(2,128)(2,1)S(1)} %all-to-all-done.1) | copy-start | bytes 3145732
  50.1 141.8 %all-to-all-start.2 = ((bf16[64,128,256]{2,0,1:T(8,128)(2,1)}), bf16[64,128,256]{2,0,1:T(8,128)(2,1)}, u32[]{:S(2)}, u32[]{:S(2)}) async-start(bf16[64,128,256]{2,0,1:T(8,128)(2,1)} %reshape_reshape.8), calls=%async_computation.2 | async-start | bytes 8388608 | tf_op jit(solution)/shard_map/all_to_all | solution.py:153
  54.7 110.3 %collective-permute-start = (bf16[1,64,256]{2,1,0:T(8,128)(2,1)S(1)}, bf16[1,64,256]{2,1,0:T(8,128)(2,1)S(1)}, u32[]{:S(2)}, u32[]{:S(2)}) collective-permute-start(bf16[1,64,256]{2,1,0:T(8,128)(2,1)S(1)} %copy-done.8), channel_id=1, source_target_pairs={{0,1},{1,0},{2,3},{3,2},{4,5},{5,4},{6,7},{7,6},{8,9},{9,8},{10,11... | collective-permute-start | bytes 98312 | tf_op jit(solution)/shard_map/ppermute | solution.py:24
  165.0 4.4 %collective-permute-start.1 = (bf16[2,64,256]{2,1,0:T(8,128)(2,1)S(1)}, bf16[2,64,256]{2,1,0:T(8,128)(2,1)S(1)}, u32[]{:S(2)}, u32[]{:S(2)}) collective-permute-start(bf16[2,64,256]{2,1,0:T(8,128)(2,1)S(1)} %pad_maximum_fusion.2), channel_id=1, source_target_pairs={{0,2},{1,3},{2,0},{3,1},{4,6},{5,7},{6,4},{7,5},{8,10},{9,11},{10,... | collective-permute-start | bytes 196616 | tf_op jit(solution)/shard_map/ppermute | solution.py:24
  169.5 8.7 %collective-permute-start.2 = (bf16[4,64,256]{2,1,0:T(8,128)(2,1)S(1)}, bf16[4,64,256]{2,1,0:T(8,128)(2,1)S(1)}, u32[]{:S(2)}, u32[]{:S(2)}) collective-permute-start(bf16[4,64,256]{2,1,0:T(8,128)(2,1)S(1)} %pad_maximum_fusion.1), channel_id=1, source_target_pairs={{0,4},{1,5},{2,6},{3,7},{4,0},{5,1},{6,2},{7,3},{8,12},{9,13},{10,... | collective-permute-start | bytes 393224 | tf_op jit(solution)/shard_map/ppermute | solution.py:24
  239.7 30.1 %all-to-all-start.3 = ((bf16[8,2,32768]{2,1,0:T(2,128)(2,1)}), bf16[8,2,32768]{2,1,0:T(2,128)(2,1)S(1)}, u32[]{:S(2)}, u32[]{:S(2)}) async-start(bf16[8,2,32768]{2,1,0:T(2,128)(2,1)} %reshape.220), calls=%async_computation.3 | async-start | bytes 2097152 | tf_op jit(solution)/shard_map/all_to_all | solution.py:174
  246.9 3.8 %copy-start.1 = (bf16[1,64,8192]{2,1,0:T(8,128)(2,1)S(1)}, bf16[1,64,8192]{2,1,0:T(8,128)(2,1)}, u32[]{:S(2)}) copy-start(bf16[1,64,8192]{2,1,0:T(8,128)(2,1)} %param.17) | copy-start | bytes 3145732
  249.2 10.2 %collective-permute-start.3 = (bf16[64,2048]{1,0:T(8,128)(2,1)S(1)}, bf16[64,2048]{1,0:T(8,128)(2,1)S(1)}, u32[]{:S(2)}, u32[]{:S(2)}) collective-permute-start(bf16[64,2048]{1,0:T(8,128)(2,1)S(1)} %convert_element_type.151), channel_id=1, source_target_pairs={{0,8},{8,16},{16,24},{24,0},{1,9},{9,17},{17,25},{25,1},{2,10},{10... | collective-permute-start | bytes 786440 | tf_op jit(solution)/shard_map/ppermute | solution.py:40
  289.5 3.6 %copy-start.2 = (bf16[1,64,8192]{2,1,0:T(8,128)(2,1)S(1)}, bf16[1,64,8192]{2,1,0:T(8,128)(2,1)}, u32[]{:S(2)}) copy-start(bf16[1,64,8192]{2,1,0:T(8,128)(2,1)} %param.17) | copy-start | bytes 3145732
  289.5 3.6 %copy-start.6 = (f32[1,8192]{1,0:T(1,128)S(1)}, f32[1,8192]{1,0:T(1,128)}, u32[]{:S(2)}) copy-start(f32[1,8192]{1,0:T(1,128)} %param.25) | copy-start | bytes 98308
